TPU v7x, 32 devices: a whole 2x2x4 slice. The times are simulated.
32 devices in a mesh: seq: 16 (over z, y, x), tp: 2 (over core).
Axes of the slice: x: 2, y: 2, z: 4, core: 2. Of those that a mesh axis runs over, the one named last changes fastest.
Arguments:
- queries: bfloat16 [1024, 8192], P('seq', 'tp'), may hold values from -8 to 8
- keys: bfloat16 [1024, 1024], P('seq', 'tp'), may hold values from -8 to 8
- values: bfloat16 [1024, 1024], P('seq', 'tp'), may hold values from -6 to 6
- segment_ids: int32 [1024], P('seq'), may hold values from 0 to 5, as said below
- out_weight: bfloat16 [8192, 16384], P('tp', 'seq'), may hold values from -0.0625 to 0.0625
Outputs:
- mixed: bfloat16 [1024, 16384], P('tp', 'seq')
Inputs may be any that keep to these rules, and one draw needn't show every extreme that they name: `segment_ids`: document ids start at 0 at the first token, never fall, and rise by at most one from a token to the next; one document covers exactly 576 tokens.
All inputs are finite; a program needn't handle non-finite values.
Results may differ from a plain program's by a relative error of at most 0.019.
Values may be sent and summed in bfloat16 or wider, within the bound.
A program may use at most 64 MiB of HBM per device.

v0:
```python
import math

import jax
import jax.numpy as jnp
from jax import lax
from jax.sharding import PartitionSpec as P

HD = 128
GROUP = 8


masked_score = -1e30


def body(queries, keys, values, segment_ids, out_weight):
    seq_rank = lax.axis_index("seq")
    tok_count = queries.shape[0]
    local_heads = keys.shape[1] // HD
    score_scale = 1.0 / math.sqrt(HD)
    all_segments = lax.all_gather(segment_ids, "seq", axis=0, tiled=True)
    offsets = jnp.arange(tok_count, dtype=jnp.int32)
    positions = seq_rank * tok_count + offsets
    query_segments = jnp.take(all_segments, positions)
    grouped = queries.reshape(tok_count, local_heads, GROUP, HD)
    key_block = lax.all_gather(keys, "seq", axis=0, tiled=True)
    value_block = lax.all_gather(values, "seq", axis=0, tiled=True)
    block_rows = key_block.shape[0]
    key_pos = jnp.arange(block_rows, dtype=jnp.int32)
    allowed = (key_pos[None, :] <= positions[:, None]) & (
        all_segments[None, :] == query_segments[:, None]
    )
    running_max = jnp.full((local_heads, tok_count, GROUP), masked_score, jnp.float32)
    key_heads = key_block.reshape(block_rows, local_heads, HD)
    value_heads = value_block.reshape(block_rows, local_heads, HD)
    scores = (
        jnp.einsum("thgd,nhd->htgn", grouped, key_heads, preferred_element_type=jnp.float32)
        * score_scale
    )
    keep_mask = allowed[None, :, None, :]
    new_max = jnp.maximum(running_max, jnp.max(jnp.where(keep_mask, scores, masked_score), axis=-1))
    weights = jnp.where(keep_mask, jnp.exp(scores - new_max[..., None]), 0.0)
    running_sum = jnp.sum(weights, axis=-1)
    summed = jnp.einsum(
        "htgn,nhd->htgd",
        weights.astype(jnp.bfloat16),
        value_heads,
        preferred_element_type=jnp.float32,
    )
    attended = (
        (summed / running_sum[..., None])
        .transpose(1, 0, 2, 3)
        .reshape(tok_count, local_heads * GROUP * HD)
    )
    attended = attended.astype(jnp.bfloat16)
    partial_out = jnp.dot(
        lax.all_gather(attended, "seq", axis=0, tiled=True),
        out_weight,
        preferred_element_type=jnp.float32,
    )
    summed_out = lax.psum_scatter(
        partial_out.astype(jnp.bfloat16), "tp", scatter_dimension=0, tiled=True
    )
    return summed_out


def solution(mesh):
    return jax.shard_map(
        body,
        mesh=mesh,
        in_specs=(P("seq", "tp"), P("seq", "tp"), P("seq", "tp"), P("seq"), P("tp", "seq")),
        out_specs=P("tp", "seq"),
        check_vma=False,
    )
```

profile of v0, /device:TPU:29, one launch (start us, length us, event | category | flops | bytes accessed | tf_op | source)
XLA Modules:
  0.0 272.9 jit_solution(8087845799112495630)
XLA Ops:
  6.5 0.0 all-gather.4.cloned.1.call-start
  6.5 0.7 all-gather.4.cloned.1.call-update
  7.3 0.0 all-gather.6.cloned.1.call-start
  7.3 0.7 all-gather.6.cloned.1.call-update
  8.0 0.0 all-gather.8.cloned.1.call-start
  8.1 1.1 copy.25
  9.2 1.2 dynamic-slice
  11.1 0.9 dynamic-update-slice
  12.0 6.5 %all-reduce = s32[1024]{0:T(1024)S(1)} all-reduce(s32[1024]{0:T(1024)S(1)} %dynamic-update-slice), channel_id=1, replica_groups=mesh['seq'=16,'tp'=2] {'seq'}, use_global_device_ids=true, to_apply=%add | all-reduce | flops 1024 | bytes 8192
  18.5 0.7 gather_fusion
  19.2 0.1 fusion.12
  19.4 44.4 %all-gather.4.cloned.1.call-done = bf16[1024,512]{1,0:T(8,128)(2,1)} async-done(((bf16[64,512]{1,0:T(8,128)(2,1)}), bf16[1024,512]{1,0:T(8,128)(2,1)}) %all-gather.4.cloned.1.call-update) | async-done | bytes 1048592 | tf_op jit(solution)/shard_map/all_gather | solution.py:25
  63.8 1.5 copy.13
  65.3 2.0 select_reduce_fusion
  67.3 0.0 copy-start
  67.3 3.2 %copy-done = f32[4,64,8,1024]{3,2,1,0:T(8,128)} copy-done((f32[4,64,8,1024]{3,2,1,0:T(8,128)}, f32[4,64,8,1024]{3,2,1,0:T(8,128)S(1)}, u32[]{:S(2)}) %copy-start) | copy-done | bytes 8388632
  70.5 2.7 fusion
  73.2 47.5 %all-gather.6.cloned.1.call-done = bf16[1024,512]{1,0:T(8,128)(2,1)} async-done(((bf16[64,512]{1,0:T(8,128)(2,1)}), bf16[1024,512]{1,0:T(8,128)(2,1)}) %all-gather.6.cloned.1.call-update) | async-done | bytes 1048592 | tf_op jit(solution)/shard_map/all_gather | solution.py:26
  120.7 1.5 copy.16
  122.2 5.4 %divide_convert_fusion = bf16[64,4,8,128]{3,2,0,1:T(8,128)(2,1)S(1)} fusion(bf16[1024,4,128,1]{0,2,3,1:T(8,128)(2,1)S(1)} %bitcast.34, f32[4,64,8,1024]{3,2,1,0:T(8,128)} %copy-done, f32[4,64,8]{2,1,0:T(8,128)S(1)} %broadcast_maximum_fusion, pred[64,1024]{1,0:T(8,128)(4,1)S(1)} %fusion.12, f32[64,4,8]{2,0,1:T(8,128)S(1)} %bitcast.36), kind=kOutput, calls=%fused_computation.9 | convolution fusion | flops 545783808 | bytes 10043392 | tf_op jit(solution)/shard_map/htgn,nhd->htgd/dot_general | solution.py:43
  127.6 0.1 copy.18
  127.7 1.0 copy.32
  128.7 0.0 all-gather.8.cloned.1.call-update
  128.7 0.0 reduce-scatter.2.cloned.1.call-start
  128.7 112.6 %all-gather.8.cloned.1.call-done = bf16[1024,4096]{1,0:T(8,128)(2,1)} async-done(((bf16[64,4096]{1,0:T(8,128)(2,1)}), bf16[1024,4096]{1,0:T(8,128)(2,1)}) %all-gather.8.cloned.1.call-update) | async-done | bytes 8388624 | tf_op jit(solution)/shard_map/all_gather | solution.py:56
  241.3 14.7 %convolution_convert_fusion = bf16[1024,1024]{1,0:T(8,128)(2,1)} fusion(bf16[1024,4096]{1,0:T(8,128)(2,1)} %all-gather.8.cloned.1.call-done, bf16[4096,1024]{1,0:T(8,128)(2,1)} %param.9), kind=kOutput, calls=%fused_computation.7 | convolution fusion | flops 8590983168 | bytes 18874368 | tf_op jit(solution)/shard_map/dot_general | solution.py:55
  256.0 0.0 reduce-scatter.2.cloned.1.call-update
  256.0 10.4 %reduce-scatter.2.cloned.1.call-done = bf16[512,1024]{1,0:T(8,128)(2,1)} async-done(((bf16[1024,1024]{1,0:T(8,128)(2,1)}), bf16[512,1024]{1,0:T(8,128)(2,1)}) %reduce-scatter.2.cloned.1.call-update) | async-done | bytes 1048592 | tf_op jit(solution)/shard_map/reduce_scatter | solution.py:60
  (6 shorter events, 0.0 us)
Async XLA Ops:
  6.5 57.3 %all-gather.4.cloned.1.call-start = ((), (), s32[]{:S(2)}) async-start(), calls=%async_computation.1 | async-start | bytes 1114112 | tf_op jit(solution)/shard_map/all_gather | solution.py:25
  7.3 113.4 %all-gather.6.cloned.1.call-start = ((), (), s32[]{:S(2)}) async-start(), calls=%async_computation.2 | async-start | bytes 1114112 | tf_op jit(solution)/shard_map/all_gather | solution.py:26
  8.0 233.3 %all-gather.8.cloned.1.call-start = ((), (), s32[]{:S(2)}) async-start(), calls=%async_computation.3 | async-start | bytes 8912896 | tf_op jit(solution)/shard_map/all_gather | solution.py:56
  67.3 3.2 %copy-start = (f32[4,64,8,1024]{3,2,1,0:T(8,128)}, f32[4,64,8,1024]{3,2,1,0:T(8,128)S(1)}, u32[]{:S(2)}) copy-start(f32[4,64,8,1024]{3,2,1,0:T(8,128)S(1)} %get-tuple-element.6) | copy-start | bytes 25165828
  128.7 137.7 %reduce-scatter.2.cloned.1.call-start = ((), (), s32[]{:S(2)}) async-start(), calls=%async_computation.4 | async-start | bytes 3145728 | tf_op jit(solution)/shard_map/reduce_scatter | solution.py:60
Sparse Core Ops, SparseCore 0:
  10.1 53.6 all-gather.3
  66.6 54.0 all-gather.5
  128.8 112.4 all-gather.7
  256.1 10.2 reduce-scatter.1
where the time goes:
time: 274 us; the launch traced here: 273 us
  waiting for transfers between devices  216 us (79%)
  matrix products  22 us (8%)
  between operations  13.9 us (5%)
  local copies, waits for them, and re-layouts  11.2 us (4%)
  blocking collectives  6.49 us (2%)
  other arithmetic  2.81 us (1%)
    all_gather x1, waiting for transfers between devices, body(): lax.all_gather(attended, 'seq', axis=0, tiled=True)  113 us
    all_gather x1, waiting for transfers between devices, body(): value_block = lax.all_gather(values, 'seq', axis=0, tiled=True)  47.5 us
    all_gather x1, waiting for transfers between devices, body(): key_block = lax.all_gather(keys, 'seq', axis=0, tiled=True)  44.4 us
    dot_general x1, matrix products, body(): jnp.dot(lax.all_gather(attended, 'seq', axis=0, tiled=True), out_weight,...  14.7 us
    reduce_scatter x1, waiting for transfers between devices, body(): lax.psum_scatter(partial_out.astype(jnp.bfloat16), 'tp', scatter_dimensio...  10.4 us
    unnamed x7, local copies, waits for them, and re-layouts  7.45 us
    unnamed x1, blocking collectives  6.49 us
  transfers between devices with their start and end apart: 4, of which 4 were waited for; matrix products, arithmetic and copies ran while one was open for 4% of the time, Pallas kernels for 0%

commit v1 on v0

--- a/solution.py
+++ b/solution.py
@@ -1,13 +1,16 @@
+import functools
 import math
 
 import jax
 import jax.numpy as jnp
 from jax import lax
+from jax.experimental import pallas as pl
+from jax.experimental.pallas import tpu as pltpu
 from jax.sharding import PartitionSpec as P
 
 HD = 128
 GROUP = 8
-
+MESH = pl.DeviceIdType.MESH
 
 masked_score = -1e30
 
@@ -63,9 +66,359 @@
     return summed_out
 
 
+NZ = 4
+TOK = 64
+LAYER = 4 * TOK
+TOKENS = NZ * LAYER
+HEADS = 4
+WIDE = GROUP * HD
+
+ROUTES = ("a", "b", "l", "a")
+
+ORDER = (
+    [("kv", 0), ("kv", 1)]
+    + [("kvz", 0, t) for t in (1, 2, 3)]
+    + [("kvn1", 0, t) for t in range(4)]
+    + [("kvn2", 0, t) for t in range(4)]
+    + [("kvz", 1, t) for t in (1, 2, 3)]
+    + [("mask",), ("attn", 0)]
+    + [("kvn1", 1, t) for t in range(4)]
+    + [("z", 0, 1)]
+    + [("kvn2", 1, t) for t in range(4)]
+    + [("attn", 1)]
+    + [("n1", 0, 0), ("z", 0, 2), ("z", 1, 1)]
+    + [("attn", 2)]
+    + [("z", 0, 3), ("n1", 0, 1), ("n1", 1, 0), ("z", 1, 2), ("l1", 2)]
+    + [("attn", 3)]
+    + [("z", 1, 3), ("z", 3, 1), ("l2", 2, 0), ("n1", 0, 2), ("n1", 1, 1), ("n1", 3, 0), ("l2", 2, 1)]
+    + [("mm", 0, 0), ("z", 3, 2), ("n1", 0, 3), ("n1", 1, 2), ("z", 3, 3), ("mm", 1, 0)]
+    + [("lz", 2, 1, 0), ("n1", 1, 3), ("n1", 3, 1), ("mm", 0, 1), ("lz", 2, 1, 1), ("n1", 3, 2)]
+    + [("lz", 2, 1, 2), ("n1", 3, 3), ("mm", 1, 1), ("lz", 2, 1, 3), ("mm", 3, 0), ("ml", 2, 0)]
+    + [("mm", 3, 1), ("ml", 2, 1)]
+    + [("n2", 0), ("mm", 0, 2), ("mm", 0, 3)]
+    + [("lz", 2, 2, w) for w in range(4)]
+    + [("n2", 1), ("mm", 1, 2), ("mm", 1, 3), ("ml", 2, 2)]
+    + [("lz", 2, 3, w) for w in range(4)]
+    + [("ml", 2, 3), ("n2", 3), ("mm", 3, 2), ("mm", 3, 3)]
+)
+
+
+def block_kernel(q_ref, k_ref, v_ref, seg_ref, w_hbm, out_ref,
+                 kv0, kv1, att, wt, acc, bias, outgoing, incoming,
+                 w_sem, send_sems, kv_sems, z_sems, p_sems, l_sems, tp_sems):
+    me = lax.axis_index("seq")
+    core = lax.axis_index("tp")
+    z = me // 4
+    w = me % 4
+    x = w % 2
+    y = w // 2
+    w_x = y * 2 + (1 - x)
+    w_y = (1 - y) * 2 + x
+    w_d = (1 - y) * 2 + (1 - x)
+    w_a = jnp.where(core == 0, w_x, w_y)
+    w_b = jnp.where(core == 0, w_y, w_x)
+    planes = {"a": (w_a, w_b), "b": (w_b, w_a), "l": (w_a, w_b)}
+
+    def nearest(t):
+        table = ((0, 1, 2, 3), (1, 0, 2, 3), (2, 3, 1, 0), (3, 2, 1, 0))
+        at = jnp.int32(table[0][t])
+        for layer in range(1, NZ):
+            at = jnp.where(z == layer, table[layer][t], at)
+        return at
+
+    layers = [z if t == 0 else nearest(t) for t in range(NZ)]
+    has_up = z < NZ - 1
+    has_down = z > 0
+    sends = []
+
+    def at_rows(layer, column):
+        return pl.ds(pl.multiple_of(layer * LAYER + column * TOK, TOK), TOK)
+
+    def copy_of(ref, recv_sem, device, send_sem):
+        return pltpu.make_async_remote_copy(
+            src_ref=ref, dst_ref=ref, send_sem=send_sem, recv_sem=recv_sem,
+            device_id=(device, core), device_id_type=MESH)
+
+    def send(ref, recv_sem, device, guard=None):
+        copy = copy_of(ref, recv_sem, device, send_sems.at[len(sends)])
+        sends.append((copy, guard))
+        if guard is None:
+            copy.start()
+        else:
+            pl.when(guard)(copy.start)
+
+    def arrive(ref, recv_sem, guard=None):
+        copy = copy_of(ref, recv_sem, me, send_sems.at[0])
+        if guard is None:
+            copy.wait_recv()
+        else:
+            pl.when(guard)(copy.wait_recv)
+
+    kvs = (kv0, kv1)
+
+    def kv_route(g):
+        return planes["a"] if g == 0 else planes["b"]
+
+    def kv_out(g, t, guard):
+        n1, n2 = kv_route(g)
+        ref = kvs[g].at[at_rows(z - t, w)]
+        if t < NZ - 1:
+            up = has_up if guard is None else jnp.logical_and(guard, has_up)
+            send(ref, kv_sems.at[g, t + 1], me + 4, up)
+        send(ref, kv_sems.at[g, 4 + t], z * 4 + n1, guard)
+        send(ref, kv_sems.at[g, 8 + t], z * 4 + n2, guard)
+
+    def kv_own(g):
+        kv_out(g, 0, None)
+
+    def kv_z(g, t):
+        guard = z >= t
+        arrive(kvs[g].at[at_rows(z - t, w)], kv_sems.at[g, t], guard)
+        kv_out(g, t, guard)
+
+    def kv_n1(g, t):
+        n1, n2 = kv_route(g)
+        guard = None if t == 0 else z >= t
+        ref = kvs[g].at[at_rows(z - t, n1)]
+        arrive(ref, kv_sems.at[g, 4 + t], guard)
+        send(ref, kv_sems.at[g, 12 + t], z * 4 + n2, guard)
+
+    def kv_n2(g, t):
+        n1, n2 = kv_route(g)
+        guard = None if t == 0 else z >= t
+        arrive(kvs[g].at[at_rows(z - t, n2)], kv_sems.at[g, 8 + t], guard)
+        arrive(kvs[g].at[at_rows(z - t, w_d)], kv_sems.at[g, 12 + t], guard)
+
+    def make_mask():
+        ones = jnp.full((8, HD), 1.0 / HD, jnp.bfloat16)
+        key_segments = lax.dot_general(
+            ones, kv0[:, 2 * HD:3 * HD], (((1,), (1,)), ((), ())),
+            preferred_element_type=jnp.float32)[0:1, :]
+        query_segments = seg_ref[:, 0:1].astype(jnp.float32)
+        key_at = lax.broadcasted_iota(jnp.int32, (TOK, TOKENS), 1)
+        query_at = me * TOK + lax.broadcasted_iota(jnp.int32, (TOK, TOKENS), 0)
+        allowed = (key_at <= query_at) & (key_segments == query_segments)
+        bias[...] = jnp.where(allowed, 0.0, masked_score)
+
+    def piece(p, layer, column):
+        return att.at[at_rows(layer, column), pl.ds(p * WIDE, WIDE)]
+
+    def z_sem(p, layer, column):
+        return z_sems.at[p, layer]
+
+    def l_sem(p, layer, c):
+        return l_sems.at[4 + c * 4 + layer]
+
+    def out_along_z(p, ref, sem):
+        send(ref, sem, me + 4, has_up)
+        send(ref, sem, me - 4, has_down)
+
+    def on_along_z(ref, sem, layer):
+        upward = layer < z
+        further = jnp.where(upward, has_up, has_down)
+        send(ref, sem, jnp.where(upward, me + 4, me - 4), further)
+
+    def attend(p):
+        kv, at, count = (kv0, 0, 1) if p == 0 else (kv1, p - 1, HEADS - 1)
+        k_cols = pl.ds(at * HD, HD)
+        v_cols = pl.ds((count + at) * HD, HD)
+        half = GROUP // 2
+
+        def heads(i, carry):
+            column = pl.multiple_of(p * WIDE + i * half * HD, HD)
+            rows = jnp.concatenate(
+                [q_ref[:, pl.ds(pl.multiple_of(column + g * HD, HD), HD)] for g in range(half)], axis=0)
+            scores = lax.dot_general(
+                rows, kv[:, k_cols], (((1,), (1,)), ((), ())),
+                preferred_element_type=jnp.float32) * (1.0 / math.sqrt(HD))
+            scores = scores.reshape(half, TOK, TOKENS) + bias[...][None]
+            weights = jnp.exp(scores - jnp.max(scores, axis=-1, keepdims=True))
+            total = jnp.sum(weights, axis=-1, keepdims=True)
+            summed = jnp.dot(
+                weights.reshape(half * TOK, TOKENS).astype(jnp.bfloat16), kv[:, v_cols],
+                preferred_element_type=jnp.float32)
+            done = (summed.reshape(half, TOK, HD) / total).astype(jnp.bfloat16)
+            for g in range(half):
+                att[at_rows(z, w), pl.ds(pl.multiple_of(column + g * HD, HD), HD)] = done[g]
+            return carry
+
+        lax.fori_loop(0, 2, heads, 0)
+        ref = piece(p, z, w)
+        n1, n2 = planes[ROUTES[p]]
+        if ROUTES[p] == "l":
+            send(ref, l_sems.at[0], z * 4 + n1)
+            send(ref, l_sems.at[1], z * 4 + n2)
+            out_along_z(p, ref, l_sem(p, z, 0))
+        else:
+            out_along_z(p, ref, z_sem(p, z, 0))
+            send(ref, p_sems.at[p, 0], z * 4 + n1)
+            send(ref, p_sems.at[p, 4], z * 4 + n2)
+
+    def from_z(p, t):
+        n1, n2 = planes[ROUTES[p]]
+        ref = piece(p, layers[t], w)
+        sem = z_sem(p, layers[t], 0)
+        arrive(ref, sem)
+        on_along_z(ref, sem, layers[t])
+        send(ref, p_sems.at[p, t], z * 4 + n1)
+        send(ref, p_sems.at[p, 4 + t], z * 4 + n2)
+
+    def from_n1(p, t):
+        n1, n2 = planes[ROUTES[p]]
+        ref = piece(p, layers[t], n1)
+        arrive(ref, p_sems.at[p, t])
+        send(ref, p_sems.at[p, 8 + t], z * 4 + n2)
+
+    def from_n2(p):
+        n1, n2 = planes[ROUTES[p]]
+        for t in range(NZ):
+            arrive(piece(p, layers[t], n2), p_sems.at[p, 4 + t])
+            arrive(piece(p, layers[t], w_d), p_sems.at[p, 8 + t])
+
+    def columns_of(p):
+        n1, n2 = planes[ROUTES[p]]
+        return (w, n1, n2, w_d)
+
+    def l_from_n1(p):
+        n1, n2 = planes[ROUTES[p]]
+        ref = piece(p, z, n1)
+        arrive(ref, l_sems.at[0])
+        send(ref, l_sems.at[2], z * 4 + n2)
+        out_along_z(p, ref, l_sem(p, z, 1))
+
+    def l_from_n2(p, c):
+        ref = piece(p, z, columns_of(p)[2 + c])
+        arrive(ref, l_sems.at[1 + c])
+        out_along_z(p, ref, l_sem(p, z, 2 + c))
+
+    def l_from_z(p, t, c):
+        ref = piece(p, layers[t], columns_of(p)[c])
+        sem = l_sem(p, layers[t], c)
+        arrive(ref, sem)
+        on_along_z(ref, sem, layers[t])
+
+    waited = []
+
+    def project(p, rows):
+        if not waited:
+            waited.append(True)
+            pltpu.make_async_copy(w_hbm, wt, w_sem).wait()
+        left = jnp.concatenate([att[r, pl.ds(p * WIDE, WIDE)] for r in rows], axis=0)
+
+        def tile(n, carry):
+            cols = pl.ds(pl.multiple_of(n * 256, 256), 256)
+            part = jnp.dot(left, wt[pl.ds(p * WIDE, WIDE), cols], preferred_element_type=jnp.float32)
+            for i, r in enumerate(rows):
+                acc[r, cols] += part[i * TOK:(i + 1) * TOK]
+            return carry
+
+        lax.fori_loop(0, acc.shape[1] // 256, tile, 0)
+
+    def project_column(p, c):
+        project(p, [at_rows(layer, columns_of(p)[c]) for layer in range(NZ)])
+
+    def project_layer(p, t):
+        project(p, [at_rows(layers[t], c) for c in range(4)])
+
+    pltpu.make_async_copy(w_hbm, wt, w_sem).start()
+    kv0[...] = jnp.zeros_like(kv0)
+    kv1[...] = jnp.zeros_like(kv1)
+    own = at_rows(z, w)
+    kv0[own, 0:HD] = k_ref[:, 0:HD]
+    kv0[own, HD:2 * HD] = v_ref[:, 0:HD]
+    kv0[own, 2 * HD:3 * HD] = seg_ref[...]
+    kv1[own, 0:3 * HD] = k_ref[:, HD:]
+    kv1[own, 3 * HD:6 * HD] = v_ref[:, HD:]
+
+    barrier = pltpu.get_barrier_semaphore()
+
+    def greet(device, at_core):
+        pl.semaphore_signal(barrier, inc=1, device_id=(device, at_core), device_id_type=MESH)
+
+    greet(me, 1 - core)
+    greet(z * 4 + w_x, core)
+    greet(z * 4 + w_y, core)
+    pl.when(has_up)(lambda: greet(me + 4, core))
+    pl.when(has_down)(lambda: greet(me - 4, core))
+    acc[...] = jnp.zeros_like(acc)
+    inner = jnp.logical_and(has_up, has_down)
+    pl.semaphore_wait(barrier, jnp.where(inner, 5, 4))
+
+    steps = {"kv": kv_own, "kvz": kv_z, "kvn1": kv_n1, "kvn2": kv_n2, "mask": make_mask,
+             "attn": attend, "z": from_z, "n1": from_n1, "n2": from_n2,
+             "l1": l_from_n1, "l2": l_from_n2, "lz": l_from_z,
+             "mm": project_column, "ml": project_layer}
+    for step in ORDER:
+        steps[step[0]](*step[1:])
+
+    half = TOKENS // 2
+    chunk = half // 4
+    copies = []
+    for i in range(4):
+        rows = pl.ds(i * chunk, chunk)
+        theirs = pl.ds(pl.multiple_of((1 - core) * half + i * chunk, chunk), chunk)
+        outgoing[rows, :] = acc[theirs, :].astype(jnp.bfloat16)
+        copy = pltpu.make_async_remote_copy(
+            src_ref=outgoing.at[rows], dst_ref=incoming.at[rows],
+            send_sem=tp_sems.at[i], recv_sem=tp_sems.at[4 + i],
+            device_id=(me, 1 - core), device_id_type=MESH)
+        copy.start()
+        copies.append(copy)
+    for copy, guard in sends:
+        if guard is None:
+            copy.wait_send()
+        else:
+            pl.when(guard)(copy.wait_send)
+    for i in range(4):
+        rows = pl.ds(i * chunk, chunk)
+        ours = pl.ds(pl.multiple_of(core * half + i * chunk, chunk), chunk)
+        copies[i].wait()
+        out_ref[rows, :] = (acc[ours, :] + incoming[rows, :].astype(jnp.float32)).astype(jnp.bfloat16)
+
+
+def count_sends():
+    each = {"kv": 3, "kvz": 3, "kvn1": 1, "z": 3, "n1": 1, "l1": 3, "l2": 2, "lz": 1, "attn": 4}
+    return sum(each.get(step[0], 0) for step in ORDER)
+
+
+def kernel_body(queries, keys, values, segment_ids, out_weight):
+    segments = jnp.broadcast_to(segment_ids.astype(jnp.bfloat16)[:, None], (TOK, HD))
+    width = out_weight.shape[1]
+    vmem = pl.BlockSpec(memory_space=pltpu.VMEM)
+    dma = pltpu.SemaphoreType.DMA
+    return pl.pallas_call(
+        block_kernel,
+        out_shape=jax.ShapeDtypeStruct((TOKENS // 2, width), jnp.bfloat16),
+        in_specs=[vmem, vmem, vmem, vmem, pl.BlockSpec(memory_space=pl.ANY)],
+        out_specs=vmem,
+        scratch_shapes=[
+            pltpu.VMEM((TOKENS, 3 * HD), jnp.bfloat16),
+            pltpu.VMEM((TOKENS, 6 * HD), jnp.bfloat16),
+            pltpu.VMEM((TOKENS, HEADS * WIDE), jnp.bfloat16),
+            pltpu.VMEM((HEADS * WIDE, width), jnp.bfloat16),
+            pltpu.VMEM((TOKENS, width), jnp.float32),
+            pltpu.VMEM((TOK, TOKENS), jnp.float32),
+            pltpu.VMEM((TOKENS // 2, width), jnp.bfloat16),
+            pltpu.VMEM((TOKENS // 2, width), jnp.bfloat16),
+            dma,
+            dma((count_sends(),)),
+            dma((2, 16)),
+            dma((HEADS, NZ)),
+            dma((HEADS, 12)),
+            dma((20,)),
+            dma((8,)),
+        ],
+        compiler_params=pltpu.CompilerParams(
+            collective_id=0, has_side_effects=True, vmem_limit_bytes=56 * 1024 * 1024),
+        cost_estimate=pl.CostEstimate(
+            flops=2 * TOKENS * HEADS * WIDE * width, bytes_accessed=16 * 2**20, transcendentals=2**21),
+    )(queries, keys, values, segments, out_weight)
+
+
 def solution(mesh):
+    fits = mesh.shape["seq"] == 4 * NZ and mesh.shape["tp"] == 2
     return jax.shard_map(
-        body,
+        kernel_body if fits else body,
         mesh=mesh,
         in_specs=(P("seq", "tp"), P("seq", "tp"), P("seq", "tp"), P("seq"), P("tp", "seq")),
         out_specs=P("tp", "seq"),

time: 274 us -> 119 us (0.43)
  waiting for transfers between devices: 216 us -> 0 us
  Pallas kernels: 0 us -> 115 us
  matrix products: 22 us -> 0 us
  between operations: 13.9 us -> 0.01 us
  local copies, waits for them, and re-layouts: 11.2 us -> 2.95 us
  blocking collectives: 6.49 us -> 0 us
    all_gather x3 -> x0, waiting for transfers between devices: 205 us -> none  [the longest x1 113 us: body(): lax.all_gather(attended, 'seq', axis=0, tiled=True)]
    pallas_call x0 -> x1, Pallas kernels: none -> 115 us  [kernel_body(): pl.pallas_call(block_kernel, out_shape=jax.ShapeDtypeStruct((TOKENS // 2,...]
    dot_general x3 -> x0, matrix products: 22 us -> none  [the longest x1 14.7 us: body(): jnp.dot(lax.all_gather(attended, 'seq', axis=0, tiled=True), out_weight,...]
    reduce_scatter x1 -> x0, waiting for transfers between devices: 10.4 us -> none  [body(): lax.psum_scatter(partial_out.astype(jnp.bfloat16), 'tp', scatter_dimensio...]
    unnamed x1 -> x0, blocking collectives: 6.49 us -> none
    unnamed x7 -> x1, local copies, waits for them, and re-layouts: 7.45 us -> 2.26 us
    all_gather x2 -> x0, local copies, waits for them, and re-layouts: 2.96 us -> none  [the longest x1 1.48 us: body(): key_block = lax.all_gather(keys, 'seq', axis=0, tiled=True)]
  transfers between devices with their start and end apart: 4 -> 0, of which waited for: 4 -> 0; matrix products, arithmetic and copies ran while one was open for 4% -> 0% of each run, Pallas kernels for 0% -> 0%
where the time goes in v1:
time: 119 us
  Pallas kernels  115 us (97%)
  local copies, waits for them, and re-layouts  2.95 us (2%)
    pallas_call x1, Pallas kernels, kernel_body(): pl.pallas_call(block_kernel, out_shape=jax.ShapeDtypeStruct((TOKENS // 2,...  115 us

profile of v1, /device:TPU:29, one launch (start us, length us, event | category | flops | bytes accessed | tf_op | source)
XLA Modules:
  0.0 118.5 jit_solution(10476742149299634964)
XLA Ops:
  0.0 0.7 convert_element_type.3
  0.7 0.7 broadcast_in_dim.2.seg_ref
  1.3 114.9 %shard_map.55 = bf16[512,1024]{1,0:T(8,128)(2,1)} custom-call(bf16[64,4096]{1,0:T(8,128)(2,1)} %q_ref.1, bf16[64,512]{1,0:T(8,128)(2,1)} %k_ref.1, bf16[64,512]{1,0:T(8,128)(2,1)} %v_ref.1, bf16[64,128]{1,0:T(8,128)(2,1)} %broadcast_in_dim.2.seg_ref, bf16[4096,1024]{1,0:T(8,128)(2,1)} %w_hbm.1), custom_call_target="tpu_custom_call" | custom-call | flops 8589934592 | bytes 16777216 | tf_op jit(solution)/shard_map/pallas_call | solution.py:389
  116.3 2.3 %copy.7 = bf16[512,1024]{1,0:T(8,128)(2,1)} copy(bf16[512,1024]{1,0:T(8,128)(2,1)} %shard_map.55) | data formatting | bytes 2097152

commit v2 on v1

--- a/solution.py
+++ b/solution.py
@@ -73,39 +73,33 @@
 HEADS = 4
 WIDE = GROUP * HD
 
-ROUTES = ("a", "b", "l", "a")
+ROUTES = ("a", "l", "b", "a")
+KV_HEADS = ((0,), (1,), (2, 3))
+KV_COLS = tuple(2 * len(heads) * HD + (HD if g == 0 else 0) for g, heads in enumerate(KV_HEADS))
+KV_GROUPS = len(KV_HEADS)
+KV_REACH = 9
 
 ORDER = (
-    [("kv", 0), ("kv", 1)]
-    + [("kvz", 0, t) for t in (1, 2, 3)]
-    + [("kvn1", 0, t) for t in range(4)]
-    + [("kvn2", 0, t) for t in range(4)]
-    + [("kvz", 1, t) for t in (1, 2, 3)]
-    + [("mask",), ("attn", 0)]
-    + [("kvn1", 1, t) for t in range(4)]
-    + [("z", 0, 1)]
-    + [("kvn2", 1, t) for t in range(4)]
-    + [("attn", 1)]
-    + [("n1", 0, 0), ("z", 0, 2), ("z", 1, 1)]
-    + [("attn", 2)]
-    + [("z", 0, 3), ("n1", 0, 1), ("n1", 1, 0), ("z", 1, 2), ("l1", 2)]
-    + [("attn", 3)]
-    + [("z", 1, 3), ("z", 3, 1), ("l2", 2, 0), ("n1", 0, 2), ("n1", 1, 1), ("n1", 3, 0), ("l2", 2, 1)]
-    + [("mm", 0, 0), ("z", 3, 2), ("n1", 0, 3), ("n1", 1, 2), ("z", 3, 3), ("mm", 1, 0)]
-    + [("lz", 2, 1, 0), ("n1", 1, 3), ("n1", 3, 1), ("mm", 0, 1), ("lz", 2, 1, 1), ("n1", 3, 2)]
-    + [("lz", 2, 1, 2), ("n1", 3, 3), ("mm", 1, 1), ("lz", 2, 1, 3), ("mm", 3, 0), ("ml", 2, 0)]
-    + [("mm", 3, 1), ("ml", 2, 1)]
-    + [("n2", 0), ("mm", 0, 2), ("mm", 0, 3)]
-    + [("lz", 2, 2, w) for w in range(4)]
-    + [("n2", 1), ("mm", 1, 2), ("mm", 1, 3), ("ml", 2, 2)]
-    + [("lz", 2, 3, w) for w in range(4)]
-    + [("ml", 2, 3), ("n2", 3), ("mm", 3, 2), ("mm", 3, 3)]
-)
+    ("kv", 0), ("kv", 1), ("kvn1", 0, 0), ("kvz", 0, 1), ("kvn1", 1, 0), ("kvz", 1, 1), ("kvz", 0, 2),
+    ("kvz", 1, 2), ("kvz", 1, 3), ("kvn1", 0, 1), ("kvn1", 0, 2), ("kv", 2), ("kvz", 0, 3), ("kvn2", 0, 0),
+    ("kvz", 2, 1), ("kvn1", 0, 3), ("kvn1", 1, 2), ("kvn1", 1, 1), ("kvn2", 1, 0), ("kvn2", 0, 3),
+    ("kvn2", 0, 1), ("kvz", 2, 2), ("kvn2", 0, 2), ("mask",), ("kvn1", 1, 3), ("attn", 0), ("kvz", 2, 3),
+    ("kvn2", 1, 1), ("kvn2", 1, 3), ("kvn2", 1, 2), ("kvn1", 2, 1), ("attn", 1), ("kvn1", 2, 0),
+    ("kvn1", 2, 3), ("kvn1", 2, 2), ("kvn2", 2, 1), ("z", 0, 1), ("z", 0, 2), ("kvn2", 2, 0), ("l1", 1),
+    ("kvn2", 2, 3), ("n1", 0, 0), ("kvn2", 2, 2), ("attn", 3), ("z", 0, 3), ("l2", 1, 1), ("n1", 0, 2),
+    ("z", 3, 1), ("lz", 1, 1, 1), ("lz", 1, 1, 0), ("z", 3, 2), ("n1", 0, 3), ("l2", 1, 0), ("n1", 0, 1),
+    ("attn", 2), ("n1", 3, 0), ("lz", 1, 2, 1), ("lz", 1, 1, 3), ("lz", 1, 2, 3), ("z", 2, 1), ("z", 3, 3),
+    ("z", 2, 2), ("lz", 1, 1, 2), ("z", 2, 3), ("n1", 3, 2), ("ml", 1, 0), ("n1", 3, 1), ("mm", 0, 0),
+    ("lz", 1, 3, 1), ("n2", 0, 0), ("n1", 3, 3), ("mm", 3, 1), ("n1", 2, 0), ("mm", 0, 2), ("lz", 1, 2, 0),
+    ("n2", 3, 0), ("mm", 2, 0), ("mm", 0, 1), ("ml", 1, 1), ("lz", 1, 2, 2), ("n2", 2, 0), ("n2", 0, 1),
+    ("ml", 1, 2), ("mm", 3, 0), ("lz", 1, 3, 3), ("n1", 2, 3), ("n1", 2, 2), ("mm", 0, 3), ("mm", 3, 2),
+    ("n1", 2, 1), ("n2", 3, 1), ("mm", 2, 1), ("lz", 1, 3, 2), ("mm", 3, 3), ("mm", 2, 2), ("lz", 1, 3, 0),
+    ("n2", 2, 1), ("mm", 2, 3), ("ml", 1, 3),)
 
 
 def block_kernel(q_ref, k_ref, v_ref, seg_ref, w_hbm, out_ref,
-                 kv0, kv1, att, wt, acc, bias, outgoing, incoming,
-                 w_sem, send_sems, kv_sems, z_sems, p_sems, l_sems, tp_sems):
+                 kv0, kv1, kv2, att, wt, acc, bias, outgoing, incoming,
+                 w_sem, send_sems, kv_sems, z_sems, p_sems, l_sems, share_sems, tp_sems):
     me = lax.axis_index("seq")
     core = lax.axis_index("tp")
     z = me // 4
@@ -154,39 +148,47 @@
         else:
             pl.when(guard)(copy.wait_recv)
 
-    kvs = (kv0, kv1)
+    kvs = (kv0, kv1, kv2)
+
+    assert (NZ - 1) * 4 - KV_REACH == 3
+    last = NZ - 1
+    at_top = z == last
 
     def kv_route(g):
-        return planes["a"] if g == 0 else planes["b"]
+        return planes["a"] if g % 2 == 0 else planes["b"]
+
+    def kv_own(g):
+        kv_out(g, 0, None)
 
     def kv_out(g, t, guard):
         n1, n2 = kv_route(g)
         ref = kvs[g].at[at_rows(z - t, w)]
-        if t < NZ - 1:
+        if t < last:
             up = has_up if guard is None else jnp.logical_and(guard, has_up)
+            if t == last - 1:
+                up = jnp.logical_and(up, w == 3)
             send(ref, kv_sems.at[g, t + 1], me + 4, up)
         send(ref, kv_sems.at[g, 4 + t], z * 4 + n1, guard)
-        send(ref, kv_sems.at[g, 8 + t], z * 4 + n2, guard)
-
-    def kv_own(g):
-        kv_out(g, 0, None)
+        if t < last:
+            send(ref, kv_sems.at[g, 8 + t], z * 4 + n2, guard)
 
     def kv_z(g, t):
-        guard = z >= t
+        guard = z >= t if t < last else jnp.logical_and(at_top, w == 3)
         arrive(kvs[g].at[at_rows(z - t, w)], kv_sems.at[g, t], guard)
         kv_out(g, t, guard)
 
     def kv_n1(g, t):
         n1, n2 = kv_route(g)
-        guard = None if t == 0 else z >= t
+        guard = None if t == 0 else z >= t if t < last else jnp.logical_and(at_top, n1 == 3)
         ref = kvs[g].at[at_rows(z - t, n1)]
         arrive(ref, kv_sems.at[g, 4 + t], guard)
         send(ref, kv_sems.at[g, 12 + t], z * 4 + n2, guard)
 
     def kv_n2(g, t):
         n1, n2 = kv_route(g)
-        guard = None if t == 0 else z >= t
-        arrive(kvs[g].at[at_rows(z - t, n2)], kv_sems.at[g, 8 + t], guard)
+        guard = None if t == 0 else z >= t if t < last else jnp.logical_and(at_top, w == 0)
+        if t < last:
+            arrive(kvs[g].at[at_rows(z - t, n2)], kv_sems.at[g, 8 + t], guard)
         arrive(kvs[g].at[at_rows(z - t, w_d)], kv_sems.at[g, 12 + t], guard)
 
     def make_mask():
@@ -194,7 +196,7 @@
         key_segments = lax.dot_general(
             ones, kv0[:, 2 * HD:3 * HD], (((1,), (1,)), ((), ())),
             preferred_element_type=jnp.float32)[0:1, :]
-        query_segments = seg_ref[:, 0:1].astype(jnp.float32)
+        query_segments = kv0[at_rows(z, w), pl.ds(2 * HD, HD)][:, 0:1].astype(jnp.float32)
         key_at = lax.broadcasted_iota(jnp.int32, (TOK, TOKENS), 1)
         query_at = me * TOK + lax.broadcasted_iota(jnp.int32, (TOK, TOKENS), 0)
         allowed = (key_at <= query_at) & (key_segments == query_segments)
@@ -219,9 +221,10 @@
         send(ref, sem, jnp.where(upward, me + 4, me - 4), further)
 
     def attend(p):
-        kv, at, count = (kv0, 0, 1) if p == 0 else (kv1, p - 1, HEADS - 1)
+        g = next(i for i, heads in enumerate(KV_HEADS) if p in heads)
+        kv, at = kvs[g], KV_HEADS[g].index(p)
         k_cols = pl.ds(at * HD, HD)
-        v_cols = pl.ds((count + at) * HD, HD)
+        v_cols = pl.ds((len(KV_HEADS[g]) + at) * HD, HD)
         half = GROUP // 2
 
         def heads(i, carry):
@@ -269,11 +272,10 @@
         arrive(ref, p_sems.at[p, t])
         send(ref, p_sems.at[p, 8 + t], z * 4 + n2)
 
-    def from_n2(p):
+    def from_n2(p, c):
         n1, n2 = planes[ROUTES[p]]
         for t in range(NZ):
-            arrive(piece(p, layers[t], n2), p_sems.at[p, 4 + t])
-            arrive(piece(p, layers[t], w_d), p_sems.at[p, 8 + t])
+            arrive(piece(p, layers[t], w_d if c else n2), p_sems.at[p, 4 + 4 * c + t])
 
     def columns_of(p):
         n1, n2 = planes[ROUTES[p]]
@@ -321,14 +323,17 @@
         project(p, [at_rows(layers[t], c) for c in range(4)])
 
     pltpu.make_async_copy(w_hbm, wt, w_sem).start()
-    kv0[...] = jnp.zeros_like(kv0)
-    kv1[...] = jnp.zeros_like(kv1)
     own = at_rows(z, w)
-    kv0[own, 0:HD] = k_ref[:, 0:HD]
-    kv0[own, HD:2 * HD] = v_ref[:, 0:HD]
-    kv0[own, 2 * HD:3 * HD] = seg_ref[...]
-    kv1[own, 0:3 * HD] = k_ref[:, HD:]
-    kv1[own, 3 * HD:6 * HD] = v_ref[:, HD:]
+    for g, heads in enumerate(KV_HEADS):
+        kvs[g][...] = jnp.zeros_like(kvs[g])
+        for i, p in enumerate(heads):
+            kvs[g][own, pl.ds(i * HD, HD)] = k_ref[:, pl.ds(p * HD, HD)]
+            kvs[g][own, pl.ds((len(heads) + i) * HD, HD)] = v_ref[:, pl.ds(p * HD, HD)]
+    square = (TOK, TOK)
+    diagonal = lax.broadcasted_iota(jnp.int32, square, 0) == lax.broadcasted_iota(jnp.int32, square, 1)
+    along = jnp.broadcast_to(seg_ref[...].astype(jnp.float32), square)
+    down = jnp.sum(jnp.where(diagonal, along, 0.0), axis=1, keepdims=True)
+    kv0[own, pl.ds(2 * HD, HD)] = jnp.broadcast_to(down, (TOK, HD)).astype(jnp.bfloat16)
 
     barrier = pltpu.get_barrier_semaphore()
 
@@ -348,32 +353,73 @@
              "attn": attend, "z": from_z, "n1": from_n1, "n2": from_n2,
              "l1": l_from_n1, "l2": l_from_n2, "lz": l_from_z,
              "mm": project_column, "ml": project_layer}
-    for step in ORDER:
-        steps[step[0]](*step[1:])
-
-    half = TOKENS // 2
-    chunk = half // 4
-    copies = []
-    for i in range(4):
-        rows = pl.ds(i * chunk, chunk)
-        theirs = pl.ds(pl.multiple_of((1 - core) * half + i * chunk, chunk), chunk)
-        outgoing[rows, :] = acc[theirs, :].astype(jnp.bfloat16)
+
+    final = final_steps()
+    mirror = {"own": "own", "A": "B", "B": "A", "D": "D"}
+    places = {"own": w, "A": w_a, "B": w_b, "D": w_d}
+    shares = []
+
+    def share_of(t, c):
+        rows = at_rows(layers[t], places[c])
+        sem = tp_sems.at[layers[t] * 4 + places[c]]
         copy = pltpu.make_async_remote_copy(
             src_ref=outgoing.at[rows], dst_ref=incoming.at[rows],
-            send_sem=tp_sems.at[i], recv_sem=tp_sems.at[4 + i],
+            send_sem=share_sems.at[4 * t + list(places).index(c)], recv_sem=sem,
             device_id=(me, 1 - core), device_id_type=MESH)
-        copy.start()
-        copies.append(copy)
+        return rows, copy, layers[t] // 2 == core
+
+    def hand_over(t, c):
+        rows, copy, ours = share_of(t, c)
+
+        def start():
+            outgoing[rows, :] = acc[rows, :].astype(jnp.bfloat16)
+            copy.start()
+
+        pl.when(jnp.logical_not(ours))(start)
+        shares.append((copy, ours))
+
+    def put_out(t, c):
+        rows, copy, ours = share_of(t, c)
+
+        def finish():
+            copy.wait_recv()
+            total = acc[rows, :] + incoming[rows, :].astype(jnp.float32)
+            at = pl.multiple_of((layers[t] - 2 * core) * LAYER + places[c] * TOK, TOK)
+            out_ref[pl.ds(at, TOK), :] = total.astype(jnp.bfloat16)
+
+        pl.when(ours)(finish)
+
+    blocks = sorted(final, key=lambda b: max(final[b], final[b[0], mirror[b[1]]]))
+    early = max(i for i, step in enumerate(ORDER) if step[0] not in ("mm", "ml"))
+    for i, step in enumerate(ORDER):
+        if i == early:
+            while blocks and max(final[blocks[0]], final[blocks[0][0], mirror[blocks[0][1]]]) < i:
+                put_out(*blocks.pop(0))
+        steps[step[0]](*step[1:])
+        for block in final:
+            if final[block] == i:
+                hand_over(*block)
+    for block in blocks:
+        put_out(*block)
+    for copy, ours in shares:
+        pl.when(jnp.logical_not(ours))(copy.wait_send)
     for copy, guard in sends:
         if guard is None:
             copy.wait_send()
         else:
             pl.when(guard)(copy.wait_send)
-    for i in range(4):
-        rows = pl.ds(i * chunk, chunk)
-        ours = pl.ds(pl.multiple_of(core * half + i * chunk, chunk), chunk)
-        copies[i].wait()
-        out_ref[rows, :] = (acc[ours, :] + incoming[rows, :].astype(jnp.float32)).astype(jnp.bfloat16)
+
+
+def final_steps():
+    final = {}
+    for i, step in enumerate(ORDER):
+        if step[0] == "mm":
+            route = ROUTES[step[1]]
+            column = ("own", "B" if route == "b" else "A", "A" if route == "b" else "B", "D")[step[2]]
+            final.update({(t, column): i for t in range(NZ)})
+        elif step[0] == "ml":
+            final.update({(step[2], column): i for column in ("own", "A", "B", "D")})
+    return final
 
 
 def count_sends():
@@ -382,7 +428,7 @@
 
 
 def kernel_body(queries, keys, values, segment_ids, out_weight):
-    segments = jnp.broadcast_to(segment_ids.astype(jnp.bfloat16)[:, None], (TOK, HD))
+    segments = segment_ids.reshape(1, TOK)
     width = out_weight.shape[1]
     vmem = pl.BlockSpec(memory_space=pltpu.VMEM)
     dma = pltpu.SemaphoreType.DMA
@@ -392,21 +438,21 @@
         in_specs=[vmem, vmem, vmem, vmem, pl.BlockSpec(memory_space=pl.ANY)],
         out_specs=vmem,
         scratch_shapes=[
-            pltpu.VMEM((TOKENS, 3 * HD), jnp.bfloat16),
-            pltpu.VMEM((TOKENS, 6 * HD), jnp.bfloat16),
+            *(pltpu.VMEM((TOKENS, cols), jnp.bfloat16) for cols in KV_COLS),
             pltpu.VMEM((TOKENS, HEADS * WIDE), jnp.bfloat16),
             pltpu.VMEM((HEADS * WIDE, width), jnp.bfloat16),
             pltpu.VMEM((TOKENS, width), jnp.float32),
             pltpu.VMEM((TOK, TOKENS), jnp.float32),
-            pltpu.VMEM((TOKENS // 2, width), jnp.bfloat16),
-            pltpu.VMEM((TOKENS // 2, width), jnp.bfloat16),
+            pltpu.VMEM((TOKENS, width), jnp.bfloat16),
+            pltpu.VMEM((TOKENS, width), jnp.bfloat16),
             dma,
             dma((count_sends(),)),
-            dma((2, 16)),
+            dma((KV_GROUPS, 16)),
             dma((HEADS, NZ)),
             dma((HEADS, 12)),
             dma((20,)),
-            dma((8,)),
+            dma((16,)),
+            dma((16,)),
         ],
         compiler_params=pltpu.CompilerParams(
             collective_id=0, has_side_effects=True, vmem_limit_bytes=56 * 1024 * 1024),

time: 119 us -> 95.2 us (0.80)
  Pallas kernels: 115 us -> 91.4 us
    pallas_call x1, Pallas kernels: 115 us -> 91.4 us  [kernel_body(): pl.pallas_call(block_kernel, out_shape=jax.ShapeDtypeStruct((TOKENS // 2,...]
where the time goes in v2:
time: 95.2 us; the launch traced here: 93.7 us
  Pallas kernels  91.4 us (96%)
  local copies, waits for them, and re-layouts  2.26 us (2%)
    pallas_call x1, Pallas kernels, kernel_body(): pl.pallas_call(block_kernel, out_shape=jax.ShapeDtypeStruct((TOKENS // 2,...  91.4 us
    unnamed x1, local copies, waits for them, and re-layouts  2.26 us

profile of v2, /device:TPU:29, one launch (start us, length us, event | category | flops | bytes accessed | tf_op | source)
XLA Modules:
  0.0 93.7 jit_solution(16432851826965023999)
XLA Ops:
  0.0 91.4 %shard_map.55 = bf16[512,1024]{1,0:T(8,128)(2,1)} custom-call(bf16[64,4096]{1,0:T(8,128)(2,1)} %q_ref.1, bf16[64,512]{1,0:T(8,128)(2,1)} %k_ref.1, bf16[64,512]{1,0:T(8,128)(2,1)} %v_ref.1, s32[1,64]{1,0:T(1,128)} %bitcast.1, bf16[4096,1024]{1,0:T(8,128)(2,1)} %w_hbm.1), custom_call_target="tpu_custom_call" | custom-call | flops 8589934592 | bytes 16777216 | tf_op jit(solution)/shard_map/pallas_call | solution.py:435
  91.4 2.3 %copy.7 = bf16[512,1024]{1,0:T(8,128)(2,1)} copy(bf16[512,1024]{1,0:T(8,128)(2,1)} %shard_map.55) | data formatting | bytes 2097152

commit v3 on v2

--- a/solution.py
+++ b/solution.py
@@ -73,28 +73,28 @@
 HEADS = 4
 WIDE = GROUP * HD
 
-ROUTES = ("a", "l", "b", "a")
-KV_HEADS = ((0,), (1,), (2, 3))
+ROUTES = ("l", "a", "b", "a")
+KV_HEADS = ((0,), (1, 2), (3,))
 KV_COLS = tuple(2 * len(heads) * HD + (HD if g == 0 else 0) for g, heads in enumerate(KV_HEADS))
 KV_GROUPS = len(KV_HEADS)
 KV_REACH = 9
 
 ORDER = (
-    ("kv", 0), ("kv", 1), ("kvn1", 0, 0), ("kvz", 0, 1), ("kvn1", 1, 0), ("kvz", 1, 1), ("kvz", 0, 2),
-    ("kvz", 1, 2), ("kvz", 1, 3), ("kvn1", 0, 1), ("kvn1", 0, 2), ("kv", 2), ("kvz", 0, 3), ("kvn2", 0, 0),
-    ("kvz", 2, 1), ("kvn1", 0, 3), ("kvn1", 1, 2), ("kvn1", 1, 1), ("kvn2", 1, 0), ("kvn2", 0, 3),
-    ("kvn2", 0, 1), ("kvz", 2, 2), ("kvn2", 0, 2), ("mask",), ("kvn1", 1, 3), ("attn", 0), ("kvz", 2, 3),
-    ("kvn2", 1, 1), ("kvn2", 1, 3), ("kvn2", 1, 2), ("kvn1", 2, 1), ("attn", 1), ("kvn1", 2, 0),
-    ("kvn1", 2, 3), ("kvn1", 2, 2), ("kvn2", 2, 1), ("z", 0, 1), ("z", 0, 2), ("kvn2", 2, 0), ("l1", 1),
-    ("kvn2", 2, 3), ("n1", 0, 0), ("kvn2", 2, 2), ("attn", 3), ("z", 0, 3), ("l2", 1, 1), ("n1", 0, 2),
-    ("z", 3, 1), ("lz", 1, 1, 1), ("lz", 1, 1, 0), ("z", 3, 2), ("n1", 0, 3), ("l2", 1, 0), ("n1", 0, 1),
-    ("attn", 2), ("n1", 3, 0), ("lz", 1, 2, 1), ("lz", 1, 1, 3), ("lz", 1, 2, 3), ("z", 2, 1), ("z", 3, 3),
-    ("z", 2, 2), ("lz", 1, 1, 2), ("z", 2, 3), ("n1", 3, 2), ("ml", 1, 0), ("n1", 3, 1), ("mm", 0, 0),
-    ("lz", 1, 3, 1), ("n2", 0, 0), ("n1", 3, 3), ("mm", 3, 1), ("n1", 2, 0), ("mm", 0, 2), ("lz", 1, 2, 0),
-    ("n2", 3, 0), ("mm", 2, 0), ("mm", 0, 1), ("ml", 1, 1), ("lz", 1, 2, 2), ("n2", 2, 0), ("n2", 0, 1),
-    ("ml", 1, 2), ("mm", 3, 0), ("lz", 1, 3, 3), ("n1", 2, 3), ("n1", 2, 2), ("mm", 0, 3), ("mm", 3, 2),
-    ("n1", 2, 1), ("n2", 3, 1), ("mm", 2, 1), ("lz", 1, 3, 2), ("mm", 3, 3), ("mm", 2, 2), ("lz", 1, 3, 0),
-    ("n2", 2, 1), ("mm", 2, 3), ("ml", 1, 3),)
+    ("kv", 0), ("kv", 1), ("kvz", 0, 1), ("kvn1", 0, 0), ("kvz", 1, 1), ("kvz", 0, 2), ("kvz", 0, 3),
+    ("kvn1", 0, 1), ("kv", 2), ("kvn1", 0, 2), ("kvz", 1, 2), ("kvz", 1, 3), ("kvn1", 1, 1), ("kvn2", 0, 0),
+    ("kvz", 2, 1), ("kvn1", 1, 0), ("kvn1", 1, 3), ("kvn2", 1, 3), ("kvz", 2, 2), ("kvn2", 0, 1),
+    ("kvn1", 0, 3), ("kvn2", 0, 2), ("kvn2", 0, 3), ("mask",), ("kvn1", 1, 2), ("attn", 0), ("kvn2", 1, 1),
+    ("kvn2", 1, 2), ("kvn1", 2, 0), ("kvn2", 1, 0), ("kvn1", 2, 2), ("kvz", 2, 3), ("l1", 0), ("kvn1", 2, 3),
+    ("attn", 2), ("l2", 0, 1), ("attn", 1), ("z", 2, 1), ("kvn2", 2, 0), ("n1", 1, 0), ("kvn1", 2, 1),
+    ("kvn2", 2, 2), ("lz", 0, 1, 3), ("l2", 0, 0), ("z", 1, 1), ("z", 2, 2), ("n1", 2, 0), ("lz", 0, 2, 3),
+    ("n1", 2, 1), ("kvn2", 2, 3), ("lz", 0, 1, 1), ("n1", 1, 1), ("z", 1, 2), ("kvn2", 2, 1), ("attn", 3),
+    ("z", 1, 3), ("z", 2, 3), ("lz", 0, 1, 2), ("lz", 0, 2, 2), ("n1", 1, 2), ("z", 3, 1), ("lz", 0, 1, 0),
+    ("z", 3, 2), ("mm", 1, 0), ("n2", 1, 0), ("z", 3, 3), ("mm", 2, 0), ("ml", 0, 0), ("n1", 2, 3),
+    ("n1", 2, 2), ("lz", 0, 2, 1), ("n1", 1, 3), ("mm", 1, 1), ("n1", 3, 1), ("mm", 1, 2), ("lz", 0, 3, 3),
+    ("n2", 2, 0), ("ml", 0, 1), ("n1", 3, 0), ("n1", 3, 3), ("lz", 0, 2, 0), ("mm", 2, 1), ("n2", 3, 0),
+    ("mm", 3, 2), ("lz", 0, 3, 1), ("ml", 0, 2), ("n1", 3, 2), ("mm", 2, 2), ("mm", 3, 1), ("n2", 2, 1),
+    ("lz", 0, 3, 0), ("mm", 2, 3), ("n2", 1, 1), ("mm", 3, 0), ("mm", 1, 3), ("lz", 0, 3, 2), ("n2", 3, 1),
+    ("mm", 3, 3), ("ml", 0, 3),)
 
 
 def block_kernel(q_ref, k_ref, v_ref, seg_ref, w_hbm, out_ref,
@@ -150,46 +150,43 @@
 
     kvs = (kv0, kv1, kv2)
 
-    assert (NZ - 1) * 4 - KV_REACH == 3
     last = NZ - 1
-    at_top = z == last
 
     def kv_route(g):
         return planes["a"] if g % 2 == 0 else planes["b"]
 
+    def reads(column, source, t):
+        blocks = 4 * t + column - source
+        return (z >= t) & (blocks >= 1) & (blocks <= KV_REACH)
+
+    def rises(t):
+        return 4 * t - w <= KV_REACH
+
     def kv_own(g):
-        kv_out(g, 0, None)
-
-    def kv_out(g, t, guard):
+        kv_out(g, 0)
+
+    def kv_out(g, t):
         n1, n2 = kv_route(g)
         ref = kvs[g].at[at_rows(z - t, w)]
         if t < last:
-            up = has_up if guard is None else jnp.logical_and(guard, has_up)
-            if t == last - 1:
-                up = jnp.logical_and(up, w == 3)
-            send(ref, kv_sems.at[g, t + 1], me + 4, up)
-        send(ref, kv_sems.at[g, 4 + t], z * 4 + n1, guard)
-        if t < last:
-            send(ref, kv_sems.at[g, 8 + t], z * 4 + n2, guard)
+            send(ref, kv_sems.at[g, t + 1], me + 4, has_up & (z >= t) & rises(t + 1))
+        send(ref, kv_sems.at[g, 4 + t], z * 4 + n1, reads(n1, w, t) | reads(w_d, w, t))
+        send(ref, kv_sems.at[g, 8 + t], z * 4 + n2, reads(n2, w, t))
 
     def kv_z(g, t):
-        guard = z >= t if t < last else jnp.logical_and(at_top, w == 3)
-        arrive(kvs[g].at[at_rows(z - t, w)], kv_sems.at[g, t], guard)
-        kv_out(g, t, guard)
+        arrive(kvs[g].at[at_rows(z - t, w)], kv_sems.at[g, t], (z >= t) & rises(t))
+        kv_out(g, t)
 
     def kv_n1(g, t):
         n1, n2 = kv_route(g)
-        guard = None if t == 0 else z >= t if t < last else jnp.logical_and(at_top, n1 == 3)
         ref = kvs[g].at[at_rows(z - t, n1)]
-        arrive(ref, kv_sems.at[g, 4 + t], guard)
-        send(ref, kv_sems.at[g, 12 + t], z * 4 + n2, guard)
+        arrive(ref, kv_sems.at[g, 4 + t], reads(w, n1, t) | reads(n2, n1, t))
+        send(ref, kv_sems.at[g, 12 + t], z * 4 + n2, reads(n2, n1, t))
 
     def kv_n2(g, t):
         n1, n2 = kv_route(g)
-        guard = None if t == 0 else z >= t if t < last else jnp.logical_and(at_top, w == 0)
-        if t < last:
-            arrive(kvs[g].at[at_rows(z - t, n2)], kv_sems.at[g, 8 + t], guard)
-        arrive(kvs[g].at[at_rows(z - t, w_d)], kv_sems.at[g, 12 + t], guard)
+        arrive(kvs[g].at[at_rows(z - t, n2)], kv_sems.at[g, 8 + t], reads(w, n2, t))
+        arrive(kvs[g].at[at_rows(z - t, w_d)], kv_sems.at[g, 12 + t], reads(w, w_d, t))
 
     def make_mask():
         ones = jnp.full((8, HD), 1.0 / HD, jnp.bfloat16)

time: 95.2 us -> 99.5 us (1.045); the launches traced: 93.7 us -> 99.4 us
  Pallas kernels: 91.4 us -> 97.1 us
    pallas_call x1, Pallas kernels: 91.4 us -> 97.1 us  [kernel_body(): pl.pallas_call(block_kernel, out_shape=jax.ShapeDtypeStruct((TOKENS // 2,...]
where the time goes in v3:
time: 99.5 us; the launch traced here: 99.4 us
  Pallas kernels  97.1 us (98%)
  local copies, waits for them, and re-layouts  2.26 us (2%)
    pallas_call x1, Pallas kernels, kernel_body(): pl.pallas_call(block_kernel, out_shape=jax.ShapeDtypeStruct((TOKENS // 2,...  97.1 us
    unnamed x1, local copies, waits for them, and re-layouts  2.26 us

profile of v3, /device:TPU:29, one launch (start us, length us, event | category | flops | bytes accessed | tf_op | source)
XLA Modules:
  0.0 99.4 jit_solution(4848030902626489872)
XLA Ops:
  0.0 97.1 %shard_map.55 = bf16[512,1024]{1,0:T(8,128)(2,1)} custom-call(bf16[64,4096]{1,0:T(8,128)(2,1)} %q_ref.1, bf16[64,512]{1,0:T(8,128)(2,1)} %k_ref.1, bf16[64,512]{1,0:T(8,128)(2,1)} %v_ref.1, s32[1,64]{1,0:T(1,128)} %bitcast.1, bf16[4096,1024]{1,0:T(8,128)(2,1)} %w_hbm.1), custom_call_target="tpu_custom_call" | custom-call | flops 8589934592 | bytes 16777216 | tf_op jit(solution)/shard_map/pallas_call | solution.py:432
  97.1 2.3 %copy.7 = bf16[512,1024]{1,0:T(8,128)(2,1)} copy(bf16[512,1024]{1,0:T(8,128)(2,1)} %shard_map.55) | data formatting | bytes 2097152
